TPU v7x, 32 devices: a whole 2x2x4 slice. The times are simulated.
32 devices in a mesh: seq: 8 (over y, x, core), head: 4 (over z).
Axes of the slice: x: 2, y: 2, z: 4, core: 2. Of those that a mesh axis runs over, the one named last changes fastest.
Arguments:
- queries: bfloat16 [16384, 512], P('seq', 'head'), may hold values from -4 to 4
- key_rows: bfloat16 [16384, 512], P('seq', 'head'), may hold values from -4 to 4
- value_rows: bfloat16 [16384, 512], P('seq', 'head'), may hold values from -6 to 6
- norm_gain: float32 [512], P('head'), may hold values from 0.1 to 1.9
- out_grad: bfloat16 [16384, 512], P('seq', 'head'), may hold values from -6 to 6
Outputs:
- normed: bfloat16 [16384, 512], P('seq', 'head')
- query_grad: bfloat16 [16384, 512], P('seq', 'head')
- key_grad: bfloat16 [16384, 512], P('seq', 'head')
- value_grad: bfloat16 [16384, 512], P('seq', 'head')
All inputs are finite; a program needn't handle non-finite values.
Results may differ from a plain program's by a relative error of at most 0.0059.
Values sent between devices are 32-bit elements; how exact they have to be, the bound alone decides.
A program may use at most 64 MiB of HBM per device.

v0:
```python
import jax
import jax.numpy as jnp
from jax import lax
from jax.sharding import PartitionSpec as P

HEAD_DIM = 128
BLOCK = 512


def causal_mask(size):
    row_index = lax.broadcasted_iota(jnp.int32, (size, size), 0)
    col_index = lax.broadcasted_iota(jnp.int32, (size, size), 1)
    return row_index >= col_index


def body(queries, key_rows, value_rows, norm_gain, out_grad):
    tokens_here = queries.shape[0]
    heads_here = queries.shape[1] // HEAD_DIM
    blocks = tokens_here // BLOCK
    block_shape = (blocks, BLOCK, heads_here, HEAD_DIM)
    query4 = queries.reshape(block_shape)
    key4 = key_rows.reshape(block_shape)
    value4 = value_rows.reshape(block_shape)
    width_all = heads_here * HEAD_DIM * lax.axis_size("head")
    mask4 = causal_mask(BLOCK)[None, None]
    position = lax.axis_index("seq")
    states = jnp.einsum("bshd,bshe->bhde", key4, value4, preferred_element_type=jnp.float32)
    totals = jnp.sum(states, 0)
    piece = lax.all_gather(totals[None], "seq", axis=0, tiled=True)
    anchor = jnp.arange(piece.shape[0], dtype=jnp.int32)
    keep = (anchor < position)[:, None, None, None]
    earlier = jnp.sum(jnp.where(keep, piece, 0.0), 0)
    running = jnp.cumsum(states, 0)
    within = jnp.concatenate([jnp.zeros_like(states[:1]), running[:-1]], 0)
    prefix16 = (earlier[None] + within).astype(jnp.bfloat16)
    scores = jnp.einsum("bthd,bshd->bhts", query4, key4, preferred_element_type=jnp.float32)
    attn = jnp.where(mask4, scores, 0.0).astype(jnp.bfloat16)
    output = jnp.einsum("bhts,bshe->bthe", attn, value4, preferred_element_type=jnp.float32)
    output = output + jnp.einsum(
        "bthd,bhde->bthe", query4, prefix16, preferred_element_type=jnp.float32
    )
    gain4 = norm_gain.reshape(heads_here, HEAD_DIM)
    scaled = out_grad.reshape(block_shape).astype(jnp.float32) * gain4
    squares, products = lax.psum(
        (jnp.sum(output * output, (2, 3)), jnp.sum(scaled * output, (2, 3))), "head"
    )
    rstd = lax.rsqrt(squares / width_all + 1e-05)[:, :, None, None]
    normed = (output * rstd * gain4).astype(jnp.bfloat16).reshape(tokens_here, -1)
    mean_prod = (products / width_all)[:, :, None, None]
    dout = (rstd * scaled - output * rstd**3 * mean_prod).astype(jnp.bfloat16)
    grad_states = jnp.einsum("bthd,bthe->bhde", query4, dout, preferred_element_type=jnp.float32)
    grad_total = jnp.sum(grad_states, 0)
    piece = lax.all_gather(grad_total[None], "seq", axis=0, tiled=True)
    anchor = jnp.arange(piece.shape[0], dtype=jnp.int32)
    keep = (anchor > position)[:, None, None, None]
    later = jnp.sum(jnp.where(keep, piece, 0.0), 0)
    behind = jnp.cumsum(grad_states[::-1], 0)[::-1]
    after = jnp.concatenate([behind[1:], jnp.zeros_like(grad_states[:1])], 0)
    suffix16 = (later[None] + after).astype(jnp.bfloat16)
    bmat = jnp.einsum("bthe,bshe->bhts", dout, value4, preferred_element_type=jnp.float32)
    bmat = jnp.where(mask4, bmat, 0.0).astype(jnp.bfloat16)
    query_grad = jnp.einsum("bhts,bshd->bthd", bmat, key4, preferred_element_type=jnp.float32)
    query_grad = query_grad + jnp.einsum(
        "bthe,bhde->bthd", dout, prefix16, preferred_element_type=jnp.float32
    )
    key_grad = jnp.einsum("bhts,bthd->bshd", bmat, query4, preferred_element_type=jnp.float32)
    key_grad = key_grad + jnp.einsum(
        "bshe,bhde->bshd", value4, suffix16, preferred_element_type=jnp.float32
    )
    value_grad = jnp.einsum("bhts,bthe->bshe", attn, dout, preferred_element_type=jnp.float32)
    value_grad = value_grad + jnp.einsum(
        "bshd,bhde->bshe", key4, suffix16, preferred_element_type=jnp.float32
    )
    return (
        normed,
        query_grad.astype(jnp.bfloat16).reshape(tokens_here, -1),
        key_grad.astype(jnp.bfloat16).reshape(tokens_here, -1),
        value_grad.astype(jnp.bfloat16).reshape(tokens_here, -1),
    )


def solution(mesh):
    return jax.shard_map(
        body,
        mesh=mesh,
        in_specs=(
            P("seq", "head"),
            P("seq", "head"),
            P("seq", "head"),
            P("head"),
            P("seq", "head"),
        ),
        out_specs=(P("seq", "head"), P("seq", "head"), P("seq", "head"), P("seq", "head")),
        check_vma=False,
    )
```

profile of v0, /device:TPU:0, one launch (start us, length us, event | category | flops | bytes accessed | tf_op | source)
XLA Modules:
  0.0 71.4 jit_solution(403312878023820120)
XLA Ops:
  0.6 0.0 copy-start
  0.7 1.0 %copy-done = bf16[2048,128]{1,0:T(8,128)(2,1)S(1)} copy-done((bf16[2048,128]{1,0:T(8,128)(2,1)S(1)}, bf16[2048,128]{1,0:T(8,128)(2,1)}, u32[]{:S(2)}) %copy-start) | copy-done | bytes 524312
  1.7 0.1 iota_compare_fusion
  1.8 0.0 copy-start.9
  1.8 1.9 %select_convert_fusion.1 = bf16[4,512,512]{2,1,0:T(8,128)(2,1)S(1)} fusion(bf16[4,512,128]{2,1,0:T(8,128)(2,1)S(1)} %bitcast.81, bf16[4,512,128]{2,1,0:T(8,128)(2,1)} %bitcast.89, pred[512,512]{1,0:T(8,128)(4,1)S(1)} %iota_compare_fusion), kind=kOutput, calls=%fused_computation.1 | convolution fusion | flops 270532608 | bytes 3407872 | tf_op jit(solution)/shard_map/bthd,bshd->bhts/dot_general | solution.py:36
  3.7 1.7 %convolution_bitcast_fusion.2 = f32[4,128,512]{1,2,0:T(8,128)} fusion(bf16[4,512,512]{2,1,0:T(8,128)(2,1)S(1)} %select_convert_fusion.1, bf16[4,512,128]{2,1,0:T(8,128)(2,1)S(1)} %bitcast.85), kind=kOutput, calls=%fused_computation.4 | convolution fusion | flops 268435456 | bytes 3670016 | tf_op jit(solution)/shard_map/bhts,bshe->bthe/dot_general | solution.py:38
  5.4 0.3 fusion.26
  5.7 12.4 %all-gather = f32[1024,128]{1,0:T(8,128)} all-gather(f32[128,128]{1,0:T(8,128)S(1)} %get-tuple-element.12), channel_id=2, replica_groups=mesh['seq'=8,'head'=4] {'seq'}, dimensions={0}, use_global_device_ids=true | all-gather | bytes 589824 | tf_op jit(solution)/shard_map/all_gather | solution.py:29
  18.1 1.3 %copy.39 = f32[8,1,128,128]{2,0,3,1:T(8,128)S(1)} copy(f32[8,1,128,128]{3,2,0,1:T(8,128)} %bitcast.93) | data formatting | bytes 1048576 | tf_op jit(solution)/shard_map/all_gather | solution.py:29
  19.4 0.2 select_reduce_fusion
  19.6 0.1 copy.40
  19.7 0.2 fusion.14
  19.9 2.8 %fusion.9 = (f32[4,512]{1,0:T(4,128)S(1)}, f32[4,512]{1,0:T(4,128)S(1)}, f32[4,512,1,128]{3,1,0,2:T(8,128)}) fusion(bf16[4,512,1,128]{3,1,0,2:T(8,128)(2,1)} %bitcast.95, f32[128]{0:T(128)S(1)} %copy-done.10, f32[4,128,512]{1,2,0:T(8,128)} %convolution_bitcast_fusion.2, bf16[4,512,128]{2,1,0:T(8,128)(2,1)S(1)} %bitcast.82, ...), kind=kOutput, calls=%fused_computation.20 | convolution fusion | flops 69070848 | bytes 3424768 | tf_op jit(solution)/shard_map/bthd,bhde->bthe/dot_general | solution.py:39
  22.7 19.0 %all-reduce.2 = (f32[4,512]{1,0:T(4,128)S(1)}, f32[4,512]{1,0:T(4,128)S(1)}) all-reduce(f32[4,512]{1,0:T(4,128)S(1)} %get-tuple-element.5, f32[4,512]{1,0:T(4,128)S(1)} %get-tuple-element.4), channel_id=1, replica_groups=mesh['seq'=8,'head'=4] {'head'}, use_global_device_ids=true, to_apply=%region_4.5 | all-reduce | flops 4096 | bytes 32768 | tf_op jit(solution)/shard_map/psum | solution.py:44
  41.7 2.8 %fusion.10 = (bf16[4,512,128]{2,1,0:T(8,128)(2,1)S(1)}, bf16[4,512,1,128]{3,1,0,2:T(8,128)(2,1)}) fusion(f32[4,512,1,128]{3,1,0,2:T(8,128)} %get-tuple-element.14, f32[4,512]{1,0:T(4,128)S(1)} %get-tuple-element.17, f32[4,512]{1,0:T(4,128)S(1)} %get-tuple-element.10, f32[128]{0:T(128)S(1)} %copy-done.10, f32[4,512]{1,0:T(4,128)S(1)} %get-tuple-element.11, ...), kind=kLoop, calls=%fused_computation.24 | loop fusion | flops 2621440 | bytes 2646528 | tf_op jit(solution)/shard_map/reshape.36
  44.5 1.5 %fusion.28 = f32[4,128,512]{2,1,0:T(8,128)} fusion(bf16[4,512,128]{2,1,0:T(8,128)(2,1)S(1)} %get-tuple-element.8, bf16[4,512,512]{2,1,0:T(8,128)(2,1)S(1)} %select_convert_fusion.1), kind=kOutput, calls=%fused_computation.47 | convolution fusion | flops 268435456 | bytes 3670016 | tf_op jit(solution)/shard_map/bhts,bthe->bshe/dot_general | solution.py:70
  46.0 1.0 %fusion.27 = (f32[128,128]{0,1:T(8,128)S(1)}, f32[4,128,128]{1,2,0:T(8,128)}) fusion(bf16[4,512,128]{2,1,0:T(8,128)(2,1)S(1)} %get-tuple-element.8, bf16[4,512,128]{2,1,0:T(8,128)(2,1)S(1)} %bitcast.84), kind=kOutput, calls=%fused_computation.46 | convolution fusion | flops 67158016 | bytes 1376256 | tf_op jit(solution)/shard_map/bthd,bthe->bhde/dot_general | solution.py:51
  47.1 11.0 %all-gather.1 = f32[1024,128]{0,1:T(8,128)S(1)} all-gather(f32[128,128]{0,1:T(8,128)S(1)} %get-tuple-element.15), channel_id=3, replica_groups=mesh['seq'=8,'head'=4] {'seq'}, dimensions={0}, use_global_device_ids=true | all-gather | bytes 589824 | tf_op jit(solution)/shard_map/all_gather | solution.py:53
  58.0 0.1 copy.59
  58.1 0.8 %fusion.11 = f32[128,128]{0,1:T(8,128)} fusion(f32[16,8,8,128]{3,2,1,0:T(8,128)S(1)} %copy.59, pred[8]{0:T(512)(128)(4,1)S(1)} %iota_compare_fusion.1), kind=kLoop, calls=%fused_computation.26 | loop fusion | flops 245760 | bytes 589832 | tf_op jit(solution)/shard_map/reduce_sum | solution.py:56
  59.0 1.0 %reverse.4 = f32[4,128,128]{1,2,0:T(8,128)S(1)} reverse(f32[4,128,128]{1,2,0:T(8,128)} %get-tuple-element.16), dimensions={0} | reverse | bytes 524288 | tf_op jit(solution)/shard_map/reverse
  59.9 0.2 fusion.12
  60.1 0.7 slice.13
  60.8 0.9 %slice.11 = f32[3,1,128,128]{2,3,0,1:T(8,128)S(1)} reverse(f32[3,1,128,128]{2,3,0,1:T(8,128)} %slice.13), dimensions={0} | reverse | bytes 393216 | tf_op jit(solution)/shard_map/slice | solution.py:58
  61.8 1.9 %fusion.4 = bf16[4,512,1,128]{1,3,0,2:T(8,128)(2,1)} fusion(f32[4,128,512]{2,1,0:T(8,128)S(1)} %copy-done.5, bf16[4,512,128]{2,1,0:T(8,128)(2,1)S(1)} %bitcast.91, f32[3,1,128,128]{2,3,0,1:T(8,128)S(1)} %slice.11, f32[128,128]{0,1:T(8,128)} %fusion.11), kind=kOutput, calls=%fused_computation.13 | convolution fusion | flops 67764224 | bytes 2359296 | tf_op jit(solution)/shard_map/bshd,bhde->bshe/dot_general | solution.py:71
  63.7 2.0 %copy.49 = bf16[4,512,1,128]{3,1,0,2:T(8,128)(2,1)} copy(bf16[4,512,1,128]{1,3,0,2:T(8,128)(2,1)} %fusion.4) | data formatting | bytes 1048576 | tf_op jit(solution)/shard_map/convert_element_type | solution.py:78
  65.8 1.7 %select_convert_fusion = bf16[4,512,512]{2,1,0:T(8,128)(2,1)S(1)} fusion(bf16[4,512,128]{2,1,0:T(8,128)(2,1)S(1)} %get-tuple-element.8, bf16[4,512,128]{2,1,0:T(8,128)(2,1)S(1)} %bitcast.87, pred[512,512]{1,0:T(8,128)(4,1)} %copy-done.9), kind=kOutput, calls=%fused_computation | convolution fusion | flops 270532608 | bytes 3407872 | tf_op jit(solution)/shard_map/bthe,bshe->bhts/dot_general | solution.py:60
  67.5 0.9 %convolution_bitcast_fusion = f32[4,128,512]{1,2,0:T(8,128)S(1)} fusion(bf16[4,512,512]{2,1,0:T(8,128)(2,1)S(1)} %select_convert_fusion, bf16[4,512,128]{2,1,0:T(8,128)(2,1)S(1)} %bitcast.83), kind=kOutput, calls=%fused_computation.2 | convolution fusion | flops 268435456 | bytes 3670016 | tf_op jit(solution)/shard_map/bhts,bthd->bshd/dot_general | solution.py:66
  68.4 1.1 %fusion.3 = bf16[4,128,512]{1,2,0:T(8,128)(2,1)} fusion(f32[4,128,512]{1,2,0:T(8,128)S(1)} %convolution_bitcast_fusion, bf16[4,512,128]{2,1,0:T(8,128)(2,1)S(1)} %bitcast.88, f32[3,1,128,128]{2,3,0,1:T(8,128)S(1)} %slice.11, f32[128,128]{0,1:T(8,128)S(1)} %copy-done.8), kind=kOutput, calls=%fused_computation.12 | convolution fusion | flops 67764224 | bytes 2359296 | tf_op jit(solution)/shard_map/bshe,bhde->bshd/dot_general | solution.py:67
  69.5 0.7 convolution_bitcast_fusion.1
  70.2 0.1 copy-done.7
  70.3 1.1 %fusion.1 = bf16[4,128,512]{1,2,0:T(8,128)(2,1)} fusion(f32[4,128,512]{1,2,0:T(8,128)S(1)} %convolution_bitcast_fusion.1, bf16[4,512,128]{2,1,0:T(8,128)(2,1)S(1)} %get-tuple-element.8, f32[3,1,128,128]{3,2,0,1:T(8,128)S(1)} %slice.12, f32[128,128]{1,0:T(8,128)S(1)} %copy-done.7), kind=kOutput, calls=%fused_computation.10 | convolution fusion | flops 67764224 | bytes 2359296 | tf_op jit(solution)/shard_map/bthe,bhde->bthd/dot_general | solution.py:63
  (22 shorter events, 0.1 us)
Async XLA Ops:
  0.6 1.0 %copy-start = (bf16[2048,128]{1,0:T(8,128)(2,1)S(1)}, bf16[2048,128]{1,0:T(8,128)(2,1)}, u32[]{:S(2)}) copy-start(bf16[2048,128]{1,0:T(8,128)(2,1)} %param.5) | copy-start | bytes 1572868
  0.6 3.0 %copy-start.1 = (bf16[2048,128]{1,0:T(8,128)(2,1)S(1)}, bf16[2048,128]{1,0:T(8,128)(2,1)}, u32[]{:S(2)}) copy-start(bf16[2048,128]{1,0:T(8,128)(2,1)} %param.7) | copy-start | bytes 1572868
  1.8 3.6 %copy-start.9 = (pred[512,512]{1,0:T(8,128)(4,1)}, pred[512,512]{1,0:T(8,128)(4,1)S(1)}, u32[]{:S(2)}) copy-start(pred[512,512]{1,0:T(8,128)(4,1)S(1)} %iota_compare_fusion) | copy-start | bytes 786436
  3.7 1.7 %copy-start.3 = (bf16[2048,128]{1,0:T(8,128)(2,1)S(1)}, bf16[2048,128]{1,0:T(8,128)(2,1)}, u32[]{:S(2)}) copy-start(bf16[2048,128]{1,0:T(8,128)(2,1)} %param.6) | copy-start | bytes 1572868
  5.4 14.5 %copy-start.10 = (f32[128]{0:T(128)S(1)}, f32[128]{0:T(128)}, u32[]{:S(2)}) copy-start(f32[128]{0:T(128)} %param.8) | copy-start | bytes 1540
  19.7 3.0 %copy-start.6 = (f32[128,128]{1,0:T(8,128)}, f32[128,128]{1,0:T(8,128)S(1)}, u32[]{:S(2)}) copy-start(f32[128,128]{1,0:T(8,128)S(1)} %copy.40) | copy-start | bytes 196612
  47.1 14.7 %copy-start.4 = (bf16[2048,128]{1,0:T(8,128)(2,1)S(1)}, bf16[2048,128]{1,0:T(8,128)(2,1)}, u32[]{:S(2)}) copy-start(bf16[2048,128]{1,0:T(8,128)(2,1)} %param.6) | copy-start | bytes 1572868
  47.1 14.7 %copy-start.5 = (f32[4,128,512]{2,1,0:T(8,128)S(1)}, f32[4,128,512]{2,1,0:T(8,128)}, u32[]{:S(2)}) copy-start(f32[4,128,512]{2,1,0:T(8,128)} %fusion.28) | copy-start | bytes 3145732
  60.1 5.6 %copy-start.2 = (bf16[2048,128]{1,0:T(8,128)(2,1)S(1)}, bf16[2048,128]{1,0:T(8,128)(2,1)}, u32[]{:S(2)}) copy-start(bf16[2048,128]{1,0:T(8,128)(2,1)} %param.7) | copy-start | bytes 1572868
  67.5 0.9 %copy-start.8 = (f32[128,128]{0,1:T(8,128)S(1)}, f32[128,128]{0,1:T(8,128)}, u32[]{:S(2)}) copy-start(f32[128,128]{0,1:T(8,128)} %fusion.11) | copy-start | bytes 196612
  69.5 0.8 %copy-start.7 = (f32[128,128]{1,0:T(8,128)S(1)}, f32[128,128]{1,0:T(8,128)}, u32[]{:S(2)}) copy-start(f32[128,128]{1,0:T(8,128)} %copy-done.6) | copy-start | bytes 196612
where the time goes:
time: 72 us; the launch traced here: 71.4 us
  blocking collectives  42.3 us (59%)
  matrix products  16.7 us (23%)
  local copies, waits for them, and re-layouts  7.31 us (10%)
  other arithmetic  4.29 us (6%)
  between operations  0.84 us (1%)
    psum x1, blocking collectives, body(): lax.psum((jnp.sum(output * output, (2, 3)), jnp.sum(scaled * output, (2,...  19 us
    all_gather x1, blocking collectives, body(): piece = lax.all_gather(totals[None], 'seq', axis=0, tiled=True)  12.4 us
    all_gather x1, blocking collectives, body(): piece = lax.all_gather(grad_total[None], 'seq', axis=0, tiled=True)  11 us
    another operation x1, other arithmetic  2.8 us
    dot_general x1, matrix products, body(): jnp.einsum('bthd,bhde->bthe', query4, prefix16, preferred_element_type=jn...  2.79 us
    convert_element_type x1, local copies, waits for them, and re-layouts, body(): value_grad.astype(jnp.bfloat16).reshape(tokens_here, -1)  2.04 us
    dot_general x1, matrix products, body(): jnp.einsum('bshd,bhde->bshe', key4, suffix16, preferred_element_type=jnp....  1.94 us
    dot_general x1, matrix products, body(): jnp.einsum('bthd,bshd->bhts', query4, key4, preferred_element_type=jnp.fl...  1.88 us

commit v1 on v0

--- a/solution.py
+++ b/solution.py
@@ -50,7 +50,12 @@
     dout = (rstd * scaled - output * rstd**3 * mean_prod).astype(jnp.bfloat16)
     grad_states = jnp.einsum("bthd,bthe->bhde", query4, dout, preferred_element_type=jnp.float32)
     grad_total = jnp.sum(grad_states, 0)
-    piece = lax.all_gather(grad_total[None], "seq", axis=0, tiled=True)
+    ring = [grad_total[None]]
+    for hop in range(7):
+        ring.append(lax.ppermute(ring[-1], "seq", [(dev, (dev + 1) % 8) for dev in range(8)]))
+    piece = jnp.roll(
+        jnp.concatenate(ring[::-1], axis=0), (lax.axis_index("seq") + 1) * ring[0].shape[0], axis=0
+    )
     anchor = jnp.arange(piece.shape[0], dtype=jnp.int32)
     keep = (anchor > position)[:, None, None, None]
     later = jnp.sum(jnp.where(keep, piece, 0.0), 0)

time: 72 us -> 78.5 us (1.090)
  waiting for transfers between devices: 0 us -> 25.8 us
  blocking collectives: 42.3 us -> 30.3 us
  local copies, waits for them, and re-layouts: 7.31 us -> 1.82 us
  matrix products: 16.7 us -> 15.1 us
    ppermute x0 -> x7, waiting for transfers between devices: none -> 25.8 us  [body(): lax.ppermute(ring[-1], 'seq', [(dev, (dev + 1) % 8) for dev in range(8)])]
    all_gather x1 -> x0, blocking collectives: 11 us -> none  [body(): piece = lax.all_gather(grad_total[None], 'seq', axis=0, tiled=True)]
    dot_general x1, matrix products: 1.94 us -> 0.3 us  [body(): jnp.einsum('bshd,bhde->bshe', key4, suffix16, preferred_element_type=jnp....]
    slice x2, local copies, waits for them, and re-layouts: 1.63 us -> 0.03 us  [body(): after = jnp.concatenate([behind[1:], jnp.zeros_like(grad_states[:1])], 0)]
    dot_general x1, matrix products: 2.79 us -> 1.42 us  [body(): jnp.einsum('bthd,bhde->bthe', query4, prefix16, preferred_element_type=jn...]
    dot_general x1, matrix products: 0.35 us -> 1.6 us  [body(): jnp.einsum('bshd,bshe->bhde', key4, value4, preferred_element_type=jnp.fl...]
    dot_general x1, matrix products: 1.09 us -> 2.3 us  [body(): jnp.einsum('bshe,bhde->bshd', value4, suffix16, preferred_element_type=jn...]
    all_gather x1, local copies, waits for them, and re-layouts: 1.27 us -> 0.19 us  [body(): piece = lax.all_gather(totals[None], 'seq', axis=0, tiled=True)]
  transfers between devices with their start and end apart: 0 -> 7, of which waited for: 0 -> 7; matrix products, arithmetic and copies ran while one was open for 0% -> 8% of each run, Pallas kernels for 0% -> 0%
where the time goes in v1:
time: 78.5 us; the launch traced here: 78.2 us
  blocking collectives  30.3 us (39%)
  waiting for transfers between devices  25.8 us (33%)
  matrix products  15.1 us (19%)
  other arithmetic  4.12 us (5%)
  local copies, waits for them, and re-layouts  1.82 us (2%)
  between operations  0.98 us (1%)
    ppermute x7, waiting for transfers between devices, body(): lax.ppermute(ring[-1], 'seq', [(dev, (dev + 1) % 8) for dev in range(8)])  25.8 us
    psum x1, blocking collectives, body(): lax.psum((jnp.sum(output * output, (2, 3)), jnp.sum(scaled * output, (2,...  19 us
    all_gather x1, blocking collectives, body(): piece = lax.all_gather(totals[None], 'seq', axis=0, tiled=True)  11.3 us
    another operation x1, other arithmetic  2.8 us
    dot_general x1, matrix products, body(): jnp.einsum('bshe,bhde->bshd', value4, suffix16, preferred_element_type=jn...  2.3 us
    dot_general x1, matrix products, body(): jnp.einsum('bhts,bthd->bshd', bmat, query4, preferred_element_type=jnp.fl...  1.9 us
    dot_general x1, matrix products, body(): jnp.einsum('bthd,bshd->bhts', query4, key4, preferred_element_type=jnp.fl...  1.75 us
    dot_general x1, matrix products, body(): jnp.einsum('bshd,bshe->bhde', key4, value4, preferred_element_type=jnp.fl...  1.6 us
  transfers between devices with their start and end apart: 7, of which 7 were waited for; matrix products, arithmetic and copies ran while one was open for 8% of the time, Pallas kernels for 0%

profile of v1, /device:TPU:0, one launch (start us, length us, event | category | flops | bytes accessed | tf_op | source)
XLA Modules:
  0.0 78.2 jit_solution(787992228840418881)
XLA Ops:
  0.6 0.0 copy-start
  0.6 0.8 iota_compare_fusion
  1.4 1.6 %fusion.25 = (f32[128,128]{1,0:T(8,128)S(1)}, f32[4,128,128]{2,1,0:T(8,128)S(1)}) fusion(bf16[4,512,128]{2,1,0:T(8,128)(2,1)} %bitcast.80, bf16[4,512,128]{2,1,0:T(8,128)(2,1)} %bitcast.84), kind=kOutput, calls=%fused_computation.60 | convolution fusion | flops 67158016 | bytes 1376256 | tf_op jit(solution)/shard_map/bshd,bshe->bhde/dot_general | solution.py:27
  3.0 0.2 fusion.13
  3.2 11.3 %all-gather = f32[1024,128]{1,0:T(8,128)S(1)} all-gather(f32[128,128]{1,0:T(8,128)S(1)} %get-tuple-element.12), channel_id=2, replica_groups=mesh['seq'=8,'head'=4] {'seq'}, dimensions={0}, use_global_device_ids=true | all-gather | bytes 589824 | tf_op jit(solution)/shard_map/all_gather | solution.py:29
  14.6 0.2 copy.50
  14.8 0.1 select_reduce_fusion.1
  14.9 0.1 copy.51
  15.0 1.7 %select_convert_fusion.1 = bf16[4,512,512]{2,1,0:T(8,128)(2,1)S(1)} fusion(bf16[4,512,128]{2,1,0:T(8,128)(2,1)S(1)} %bitcast.76, bf16[4,512,128]{2,1,0:T(8,128)(2,1)S(1)} %bitcast.81, pred[512,512]{1,0:T(8,128)(4,1)} %iota_compare_fusion), kind=kOutput, calls=%fused_computation.1 | convolution fusion | flops 270532608 | bytes 3407872 | tf_op jit(solution)/shard_map/bthd,bshd->bhts/dot_general | solution.py:36
  16.8 0.7 convolution_bitcast_fusion.2
  17.5 0.3 copy-done.6
  17.8 1.4 %fusion.9 = (f32[4,512]{1,0:T(4,128)S(1)}, f32[4,512]{1,0:T(4,128)S(1)}, f32[4,512,1,128]{3,1,0,2:T(8,128)}) fusion(bf16[4,512,1,128]{3,1,0,2:T(8,128)(2,1)S(1)} %bitcast.89, f32[128]{0:T(128)S(1)} %copy-done.9, f32[4,128,512]{1,2,0:T(8,128)S(1)} %convolution_bitcast_fusion.2, bf16[4,512,128]{2,1,0:T(8,128)(2,1)S(1)} %bitcast.77, ...), kind=kOutput, calls=%fused_computation.20 | convolution fusion | flops 69070848 | bytes 3424768 | tf_op jit(solution)/shard_map/bthd,bhde->bthe/dot_general | solution.py:39
  19.2 19.0 %all-reduce.2 = (f32[4,512]{1,0:T(4,128)S(1)}, f32[4,512]{1,0:T(4,128)S(1)}) all-reduce(f32[4,512]{1,0:T(4,128)S(1)} %get-tuple-element.5, f32[4,512]{1,0:T(4,128)S(1)} %get-tuple-element.4), channel_id=1, replica_groups=mesh['seq'=8,'head'=4] {'head'}, use_global_device_ids=true, to_apply=%region_4.5 | all-reduce | flops 4096 | bytes 32768 | tf_op jit(solution)/shard_map/psum | solution.py:44
  38.2 2.8 %fusion.10 = (bf16[4,512,128]{2,1,0:T(8,128)(2,1)S(1)}, bf16[4,512,1,128]{3,1,0,2:T(8,128)(2,1)}) fusion(f32[4,512,1,128]{3,1,0,2:T(8,128)} %get-tuple-element.14, f32[4,512]{1,0:T(4,128)S(1)} %get-tuple-element.17, f32[4,512]{1,0:T(4,128)S(1)} %get-tuple-element.10, f32[128]{0:T(128)S(1)} %copy-done.9, f32[4,512]{1,0:T(4,128)S(1)} %get-tuple-element.11, ...), kind=kLoop, calls=%fused_computation.24 | loop fusion | flops 2621440 | bytes 2646528 | tf_op jit(solution)/shard_map/reshape.36
  41.0 1.1 %fusion.26 = (f32[128,128]{0,1:T(8,128)S(1)}, f32[4,128,128]{1,2,0:T(8,128)}) fusion(bf16[4,512,128]{2,1,0:T(8,128)(2,1)S(1)} %get-tuple-element.8, bf16[4,512,128]{2,1,0:T(8,128)(2,1)S(1)} %bitcast.79), kind=kOutput, calls=%fused_computation.61 | convolution fusion | flops 67158016 | bytes 1376256 | tf_op jit(solution)/shard_map/bthd,bthe->bhde/dot_general | solution.py:51
  42.1 1.5 %fusion.27 = f32[4,128,512]{2,1,0:T(8,128)} fusion(bf16[4,512,128]{2,1,0:T(8,128)(2,1)S(1)} %get-tuple-element.8, bf16[4,512,512]{2,1,0:T(8,128)(2,1)S(1)} %select_convert_fusion.1), kind=kOutput, calls=%fused_computation.62 | convolution fusion | flops 268435456 | bytes 3670016 | tf_op jit(solution)/shard_map/bhts,bthe->bshe/dot_general | solution.py:75
  43.7 3.1 %collective-permute-done = f32[1,1,128,128]{2,3,1,0:T(8,128)S(1)} collective-permute-done((f32[1,1,128,128]{2,3,1,0:T(8,128)S(1)}, f32[1,1,128,128]{2,3,1,0:T(8,128)S(1)}, u32[]{:S(2)}, u32[]{:S(2)}) %collective-permute-start) | collective-permute-done | bytes 65568 | tf_op jit(solution)/shard_map/ppermute | solution.py:55
  46.7 0.8 select_convert_fusion
  47.5 3.8 %collective-permute-done.1 = f32[1,1,128,128]{2,3,1,0:T(8,128)S(1)} collective-permute-done((f32[1,1,128,128]{2,3,1,0:T(8,128)S(1)}, f32[1,1,128,128]{2,3,1,0:T(8,128)S(1)}, u32[]{:S(2)}, u32[]{:S(2)}) %collective-permute-start.1) | collective-permute-done | bytes 65568 | tf_op jit(solution)/shard_map/ppermute | solution.py:55
  51.3 1.9 %convolution_bitcast_fusion = f32[4,128,512]{1,2,0:T(8,128)} fusion(bf16[4,512,512]{2,1,0:T(8,128)(2,1)S(1)} %select_convert_fusion, bf16[4,512,128]{2,1,0:T(8,128)(2,1)S(1)} %bitcast.78), kind=kOutput, calls=%fused_computation.2 | convolution fusion | flops 268435456 | bytes 3670016 | tf_op jit(solution)/shard_map/bhts,bthd->bshd/dot_general | solution.py:71
  53.2 2.7 %collective-permute-done.2 = f32[1,1,128,128]{2,3,1,0:T(8,128)S(1)} collective-permute-done((f32[1,1,128,128]{2,3,1,0:T(8,128)S(1)}, f32[1,1,128,128]{2,3,1,0:T(8,128)S(1)}, u32[]{:S(2)}, u32[]{:S(2)}) %collective-permute-start.2) | collective-permute-done | bytes 65568 | tf_op jit(solution)/shard_map/ppermute | solution.py:55
  55.9 0.7 convolution_bitcast_fusion.1
  56.6 3.9 %collective-permute-done.3 = f32[1,1,128,128]{2,3,1,0:T(8,128)S(1)} collective-permute-done((f32[1,1,128,128]{2,3,1,0:T(8,128)S(1)}, f32[1,1,128,128]{2,3,1,0:T(8,128)S(1)}, u32[]{:S(2)}, u32[]{:S(2)}) %collective-permute-start.3) | collective-permute-done | bytes 65568 | tf_op jit(solution)/shard_map/ppermute | solution.py:55
  60.5 1.1 %fusion.1 = bf16[4,128,512]{1,2,0:T(8,128)(2,1)} fusion(f32[4,128,512]{1,2,0:T(8,128)S(1)} %convolution_bitcast_fusion.1, bf16[4,512,128]{2,1,0:T(8,128)(2,1)S(1)} %get-tuple-element.8, f32[3,1,128,128]{3,2,0,1:T(8,128)S(1)} %slice.12, f32[128,128]{1,0:T(8,128)S(1)} %copy.51), kind=kOutput, calls=%fused_computation.10 | convolution fusion | flops 67764224 | bytes 2359296 | tf_op jit(solution)/shard_map/bthe,bhde->bthd/dot_general | solution.py:68
  61.6 3.5 %collective-permute-done.4 = f32[1,1,128,128]{2,3,1,0:T(8,128)S(1)} collective-permute-done((f32[1,1,128,128]{2,3,1,0:T(8,128)S(1)}, f32[1,1,128,128]{2,3,1,0:T(8,128)S(1)}, u32[]{:S(2)}, u32[]{:S(2)}) %collective-permute-start.4) | collective-permute-done | bytes 65568 | tf_op jit(solution)/shard_map/ppermute | solution.py:55
  65.1 0.1 fusion.11
  65.3 4.4 %collective-permute-done.5 = f32[1,1,128,128]{2,3,1,0:T(8,128)S(1)} collective-permute-done((f32[1,1,128,128]{2,3,1,0:T(8,128)S(1)}, f32[1,1,128,128]{2,3,1,0:T(8,128)S(1)}, u32[]{:S(2)}, u32[]{:S(2)}) %collective-permute-start.5) | collective-permute-done | bytes 65568 | tf_op jit(solution)/shard_map/ppermute | solution.py:55
  69.7 4.6 %collective-permute-done.6 = f32[1,1,128,128]{2,3,1,0:T(8,128)S(1)} collective-permute-done((f32[1,1,128,128]{2,3,1,0:T(8,128)S(1)}, f32[1,1,128,128]{2,3,1,0:T(8,128)S(1)}, u32[]{:S(2)}, u32[]{:S(2)}) %collective-permute-start.6) | collective-permute-done | bytes 65568 | tf_op jit(solution)/shard_map/ppermute | solution.py:55
  74.5 0.1 select_reduce_fusion
  74.6 0.3 fusion.4
  74.9 1.0 %copy.60 = bf16[4,512,1,128]{3,1,0,2:T(8,128)(2,1)} copy(bf16[4,512,1,128]{1,3,0,2:T(8,128)(2,1)S(1)} %fusion.4) | data formatting | bytes 1048576 | tf_op jit(solution)/shard_map/convert_element_type | solution.py:83
  75.9 2.3 %fusion.3 = bf16[4,128,512]{1,2,0:T(8,128)(2,1)} fusion(f32[4,128,512]{1,2,0:T(8,128)} %convolution_bitcast_fusion, bf16[4,512,128]{2,1,0:T(8,128)(2,1)S(1)} %bitcast.87, f32[3,1,128,128]{2,3,0,1:T(8,128)S(1)} %slice.11, f32[128,128]{0,1:T(8,128)S(1)} %select_reduce_fusion), kind=kOutput, calls=%fused_computation.12 | convolution fusion | flops 67764224 | bytes 2359296 | tf_op jit(solution)/shard_map/bshe,bhde->bshd/dot_general | solution.py:72
  (48 shorter events, 0.3 us)
Async XLA Ops:
  0.6 14.3 %copy-start = (bf16[2048,128]{1,0:T(8,128)(2,1)S(1)}, bf16[2048,128]{1,0:T(8,128)(2,1)}, u32[]{:S(2)}) copy-start(bf16[2048,128]{1,0:T(8,128)(2,1)} %param.5) | copy-start | bytes 1572868
  1.4 13.5 %copy-start.1 = (bf16[2048,128]{1,0:T(8,128)(2,1)S(1)}, bf16[2048,128]{1,0:T(8,128)(2,1)}, u32[]{:S(2)}) copy-start(bf16[2048,128]{1,0:T(8,128)(2,1)} %param.6) | copy-start | bytes 1572868
  15.0 1.8 %copy-start.2 = (bf16[2048,128]{1,0:T(8,128)(2,1)S(1)}, bf16[2048,128]{1,0:T(8,128)(2,1)}, u32[]{:S(2)}) copy-start(bf16[2048,128]{1,0:T(8,128)(2,1)} %param.7) | copy-start | bytes 1572868
  16.8 1.0 %copy-start.6 = (bf16[2048,128]{1,0:T(8,128)(2,1)S(1)}, bf16[2048,128]{1,0:T(8,128)(2,1)}, u32[]{:S(2)}) copy-start(bf16[2048,128]{1,0:T(8,128)(2,1)} %param.9) | copy-start | bytes 1572868
  16.8 1.0 %copy-start.9 = (f32[128]{0:T(128)S(1)}, f32[128]{0:T(128)}, u32[]{:S(2)}) copy-start(f32[128]{0:T(128)} %param.8) | copy-start | bytes 1540
  42.1 4.6 %copy-start.3 = (bf16[2048,128]{1,0:T(8,128)(2,1)S(1)}, bf16[2048,128]{1,0:T(8,128)(2,1)}, u32[]{:S(2)}) copy-start(bf16[2048,128]{1,0:T(8,128)(2,1)} %param.7) | copy-start | bytes 1572868
  42.1 4.6 %copy-start.8 = (pred[512,512]{1,0:T(8,128)(4,1)S(1)}, pred[512,512]{1,0:T(8,128)(4,1)}, u32[]{:S(2)}) copy-start(pred[512,512]{1,0:T(8,128)(4,1)} %iota_compare_fusion) | copy-start | bytes 786436
  42.1 4.6 %collective-permute-start = (f32[1,1,128,128]{2,3,1,0:T(8,128)S(1)}, f32[1,1,128,128]{2,3,1,0:T(8,128)S(1)}, u32[]{:S(2)}, u32[]{:S(2)}) collective-permute-start(f32[1,1,128,128]{2,3,1,0:T(8,128)S(1)} %bitcast.90), channel_id=1, source_target_pairs={{0,4},{4,8},{8,12},{12,16},{16,20},{20,24},{24,28},{28,0},{1,5},{5... | collective-permute-start | bytes 196616 | tf_op jit(solution)/shard_map/ppermute | solution.py:55
  46.7 4.6 %collective-permute-start.1 = (f32[1,1,128,128]{2,3,1,0:T(8,128)S(1)}, f32[1,1,128,128]{2,3,1,0:T(8,128)S(1)}, u32[]{:S(2)}, u32[]{:S(2)}) collective-permute-start(f32[1,1,128,128]{2,3,1,0:T(8,128)S(1)} %collective-permute-done), channel_id=1, source_target_pairs={{0,4},{4,8},{8,12},{12,16},{16,20},{20,24},{24,28},{28,0},{1,5},{5... | collective-permute-start | bytes 196616 | tf_op jit(solution)/shard_map/ppermute | solution.py:55
  51.3 4.6 %collective-permute-start.2 = (f32[1,1,128,128]{2,3,1,0:T(8,128)S(1)}, f32[1,1,128,128]{2,3,1,0:T(8,128)S(1)}, u32[]{:S(2)}, u32[]{:S(2)}) collective-permute-start(f32[1,1,128,128]{2,3,1,0:T(8,128)S(1)} %collective-permute-done.1), channel_id=1, source_target_pairs={{0,4},{4,8},{8,12},{12,16},{16,20},{20,24},{24,28},{28,0},{1,5},{5... | collective-permute-start | bytes 196616 | tf_op jit(solution)/shard_map/ppermute | solution.py:55
  55.9 4.6 %collective-permute-start.3 = (f32[1,1,128,128]{2,3,1,0:T(8,128)S(1)}, f32[1,1,128,128]{2,3,1,0:T(8,128)S(1)}, u32[]{:S(2)}, u32[]{:S(2)}) collective-permute-start(f32[1,1,128,128]{2,3,1,0:T(8,128)S(1)} %collective-permute-done.2), channel_id=1, source_target_pairs={{0,4},{4,8},{8,12},{12,16},{16,20},{20,24},{24,28},{28,0},{1,5},{5... | collective-permute-start | bytes 196616 | tf_op jit(solution)/shard_map/ppermute | solution.py:55
  56.6 5.0 %copy-start.7 = (f32[4,128,128]{1,2,0:T(8,128)S(1)}, f32[4,128,128]{1,2,0:T(8,128)}, u32[]{:S(2)}) copy-start(f32[4,128,128]{1,2,0:T(8,128)} %get-tuple-element.16) | copy-start | bytes 786436
  60.5 4.6 %collective-permute-start.4 = (f32[1,1,128,128]{2,3,1,0:T(8,128)S(1)}, f32[1,1,128,128]{2,3,1,0:T(8,128)S(1)}, u32[]{:S(2)}, u32[]{:S(2)}) collective-permute-start(f32[1,1,128,128]{2,3,1,0:T(8,128)S(1)} %collective-permute-done.3), channel_id=1, source_target_pairs={{0,4},{4,8},{8,12},{12,16},{16,20},{20,24},{24,28},{28,0},{1,5},{5... | collective-permute-start | bytes 196616 | tf_op jit(solution)/shard_map/ppermute | solution.py:55
  61.6 13.0 %copy-start.5 = (f32[4,128,512]{2,1,0:T(8,128)S(1)}, f32[4,128,512]{2,1,0:T(8,128)}, u32[]{:S(2)}) copy-start(f32[4,128,512]{2,1,0:T(8,128)} %fusion.27) | copy-start | bytes 3145732
  65.1 4.6 %collective-permute-start.5 = (f32[1,1,128,128]{2,3,1,0:T(8,128)S(1)}, f32[1,1,128,128]{2,3,1,0:T(8,128)S(1)}, u32[]{:S(2)}, u32[]{:S(2)}) collective-permute-start(f32[1,1,128,128]{2,3,1,0:T(8,128)S(1)} %collective-permute-done.4), channel_id=1, source_target_pairs={{0,4},{4,8},{8,12},{12,16},{16,20},{20,24},{24,28},{28,0},{1,5},{5... | collective-permute-start | bytes 196616 | tf_op jit(solution)/shard_map/ppermute | solution.py:55
  69.7 4.6 %collective-permute-start.6 = (f32[1,1,128,128]{2,3,1,0:T(8,128)S(1)}, f32[1,1,128,128]{2,3,1,0:T(8,128)S(1)}, u32[]{:S(2)}, u32[]{:S(2)}) collective-permute-start(f32[1,1,128,128]{2,3,1,0:T(8,128)S(1)} %collective-permute-done.5), channel_id=1, source_target_pairs={{0,4},{4,8},{8,12},{12,16},{16,20},{20,24},{24,28},{28,0},{1,5},{5... | collective-permute-start | bytes 196616 | tf_op jit(solution)/shard_map/ppermute | solution.py:55
  74.5 1.5 %copy-start.4 = (bf16[2048,128]{1,0:T(8,128)(2,1)S(1)}, bf16[2048,128]{1,0:T(8,128)(2,1)}, u32[]{:S(2)}) copy-start(bf16[2048,128]{1,0:T(8,128)(2,1)} %param.7) | copy-start | bytes 1572868
